TPU v7x, 32 devices: a whole 2x2x4 slice. The times are simulated.
32 devices in a mesh: groups: 2 (over y), expert: 4 (over z), dp: 4 (over x, core).
Axes of the slice: x: 2, y: 2, z: 4, core: 2. Of those that a mesh axis runs over, the one named last changes fastest.
Arguments:
- tokens: bfloat16 [128, 7168], P(('groups', 'expert', 'dp')), parts along dimension 0, may hold values from -6 to 6
- routes: int32 [128, 8], P(('groups', 'expert', 'dp')), parts along dimension 0, may hold values from 0 to 15, as said below
- combine_weight: bfloat16 [128, 8], P(('groups', 'expert', 'dp')), parts along dimension 0, may hold values from 0.049804688 to 0.59765625
- live_rows: int32 [32], P(('groups', 'expert', 'dp')), parts along dimension 0, may hold values from 1 to 4, as said below
- gate_projection_weight: bfloat16 [16, 7168, 2048], P('expert', None, 'dp'), may hold values from -0.0625 to 0.0625
- up_projection_weight: bfloat16 [16, 7168, 2048], P('expert', None, 'dp'), may hold values from -0.0625 to 0.0625
- down_projection_weight: bfloat16 [16, 2048, 7168], P('expert', 'dp'), may hold values from -0.125 to 0.125
Outputs:
- mixed: bfloat16 [128, 7168], P(('groups', 'expert', 'dp')), parts along dimension 0
There are 2 independent parts, one for each index of `groups`. A program takes and returns all parts, laid end to end along the dimension named above; an argument that names none is the same for every part. Nothing has to cross between parts.
Inputs may be any that keep to these rules, and one draw needn't show every extreme that they name: `routes`: each row names 8 different experts; in each aligned block of 16 rows every expert is named by at least one row and no expert by more than 12 rows, and one expert by exactly 12. `live_rows`: entry i counts the live rows, the first ones, of the i-th block of 4 rows; all devices of some aligned block of 16 rows have all 4 rows live.
All inputs are finite; a program needn't handle non-finite values.
Results may differ from a plain program's by a relative error of at most 0.011.
Values may be sent and summed in bfloat16 or wider, within the bound.
A program may use at most 192 MiB of HBM per device.

v0:
```python
import functools

import jax
import jax.numpy as jnp
from jax import lax
from jax.experimental import pallas as pl
from jax.experimental.pallas import tpu as pltpu
from jax.sharding import PartitionSpec as P

SLAB = 16
CHUNK = 512
LANES = 128
LAG = 2
MESH = pl.DeviceIdType.MESH


def kernel(
    n_x,
    n_z,
    depth,
    tokens,
    routes,
    combine,
    live,
    gate_w,
    up_w,
    down_w,
    out,
    gathered,
    rows,
    table,
    hidden,
    gate_acc,
    up_acc,
    gu_ring,
    down_buf,
    own_a,
    send_a,
    recv_a,
    own_x,
    send_x,
    recv_x,
    send_z,
    recv_z,
    gu_sem,
    down_sem,
    gz_send,
    gz_recv,
    gx_send,
    gx_recv,
    gc_send,
    gc_recv,
    a_ssem,
    a_rsem,
    x_ssem,
    x_rsem,
    z_ssem,
    z_rsem,
):
    f32, bf16 = jnp.float32, jnp.bfloat16
    tok, width = tokens.shape
    top = routes.shape[1]
    local_count, ff = gate_w.shape[0], gate_w.shape[2]
    quarters = SLAB // tok
    part = width // quarters
    count = width // CHUNK
    piece = CHUNK // quarters
    chip_rows = n_z * tok
    half = n_x * chip_rows
    total = 2 * half

    z = lax.axis_index("expert")
    dp = lax.axis_index("dp")
    core = lax.rem(dp, 2)
    x = lax.div(dp, 2)
    sibling = {"dp": x * 2 + 1 - core}

    def x_peer(dx):
        return {"dp": lax.rem(x + dx, n_x) * 2 + core}

    def z_peer(dz):
        return {"expert": lax.rem(z + dz, n_z)}

    def slab(c, dx, dz):
        return gathered.at[pl.ds(((c * n_x + dx) * n_z + dz) * SLAB, SLAB), :]

    barrier = pltpu.get_barrier_semaphore()
    peers = [sibling]
    peers += [x_peer(dx) for dx in range(1, n_x)]
    peers += [z_peer(dz) for dz in range(1, n_z)]
    for peer in peers:
        pl.semaphore_signal(barrier, inc=1, device_id=peer, device_id_type=MESH)

    def gu_copy(e, q, which):
        place = lax.rem(e, depth)
        return pltpu.make_async_copy(
            (gate_w, up_w)[which].at[e, pl.ds(q * part, part), :],
            gu_ring.at[place, q, which],
            gu_sem.at[place, q, which],
        )

    def down_copy(c):
        return pltpu.make_async_copy(
            down_w.at[:, :, pl.ds(pl.multiple_of(c * CHUNK, CHUNK), CHUNK)],
            down_buf.at[c],
            down_sem.at[c],
        )

    for e in range(depth):
        for q in range(quarters):
            for which in range(2):
                gu_copy(e, q, which).start()

    wide = tokens[...].astype(f32)
    packed = jnp.concatenate([wide[:, q * part : (q + 1) * part] for q in range(quarters)], axis=0)
    gathered[0:SLAB, 0:part] = packed.astype(bf16)
    lane = lax.broadcasted_iota(jnp.int32, (tok, LANES), 1)
    row = lax.broadcasted_iota(jnp.int32, (tok, LANES), 0)
    chosen = routes[...]
    share = combine[...].astype(f32)
    weights = jnp.zeros((tok, LANES), f32)
    for k in range(top):
        weights += jnp.where(chosen[:, k : k + 1] == lane, share[:, k : k + 1], 0.0)
    weights = jnp.where(row < live[0], weights, 0.0)
    gathered[0:SLAB, part : part + LANES] = jnp.concatenate([weights] * quarters, axis=0).astype(bf16)

    pl.semaphore_wait(barrier, len(peers))

    def gz(dz):
        return pltpu.make_async_remote_copy(
            src_ref=slab(0, 0, 0),
            dst_ref=slab(0, 0, n_z - dz),
            send_sem=gz_send.at[dz],
            recv_sem=gz_recv.at[n_z - dz],
            device_id=z_peer(dz),
            device_id_type=MESH,
        )

    def gx(dx, dz):
        return pltpu.make_async_remote_copy(
            src_ref=slab(0, 0, dz),
            dst_ref=slab(0, n_x - dx, dz),
            send_sem=gx_send.at[dx, dz],
            recv_sem=gx_recv.at[n_x - dx, dz],
            device_id=x_peer(dx),
            device_id_type=MESH,
        )

    def gc(dx, dz):
        return pltpu.make_async_remote_copy(
            src_ref=slab(0, dx, dz),
            dst_ref=slab(1, dx, dz),
            send_sem=gc_send.at[dx, dz],
            recv_sem=gc_recv.at[dx, dz],
            device_id=sibling,
            device_id_type=MESH,
        )

    order = sorted(range(1, n_z), key=lambda dz: (min(dz, n_z - dz), dz))
    for dz in order:
        gz(dz).start()
    for dz in [0] + order:
        if dz:
            gz(n_z - dz).wait_recv()
        for dx in range(1, n_x):
            gx(dx, dz).start()
        gc(0, dz).start()
    for dz in [0] + order:
        for dx in range(1, n_x):
            gx(n_x - dx, dz).wait_recv()
            gc(dx, dz).start()
    for dz in [0] + order:
        for dx in range(n_x):
            gc(dx, dz).wait_recv()
    for dz in range(n_z):
        if dz:
            gz(dz).wait_send()
        for dx in range(n_x):
            if dx:
                gx(dx, dz).wait_send()
            gc(dx, dz).wait_send()

    to = lax.broadcasted_iota(jnp.int32, (total, total * quarters), 0)
    came = lax.broadcasted_iota(jnp.int32, (total, total * quarters), 1)
    first = lax.div(to, tok) * SLAB + lax.rem(to, tok)
    for q in range(quarters):
        pick = jnp.where(came == first + q * tok, 1.0, 0.0).astype(bf16)
        rows[q] = jnp.dot(pick, gathered[:, 0:part], preferred_element_type=f32).astype(bf16)
        if q == 0:
            table[...] = jnp.dot(pick, gathered[:, part : part + LANES], preferred_element_type=f32)

    spread = -(-count // (depth * quarters))

    def expert(e, _):
        place = lax.rem(e, depth)
        for q in range(quarters):
            for which, acc in ((0, gate_acc), (1, up_acc)):
                gu_copy(e, q, which).wait()
                term = jnp.dot(rows[q], gu_ring[place, q, which], preferred_element_type=f32)
                if q == 0:
                    acc[...] = term
                else:
                    acc[...] += term

            @pl.when(e + depth < local_count)
            def _():
                for which in range(2):
                    gu_copy(e + depth, q, which).start()

            @pl.when(e + depth >= local_count)
            def _():
                begin = ((e + depth - local_count) * quarters + q) * spread
                for k in range(spread):

                    @pl.when(begin + k < count)
                    def _():
                        down_copy(begin + k).start()

        lanes = lax.broadcasted_iota(jnp.int32, (total, LANES), 1)
        mine = jnp.where(lanes == z * local_count + e, table[...], 0.0)
        weight = jnp.sum(mine, axis=1, keepdims=True)
        g = gate_acc[...]
        value = g / (1.0 + jnp.exp(-g)) * up_acc[...] * weight
        hidden[:, pl.ds(pl.multiple_of(e * ff, LANES), ff)] = value.astype(bf16)
        return 0

    lax.fori_loop(0, local_count, expert, 0)

    def cp_a(c):
        return pltpu.make_async_remote_copy(
            src_ref=send_a.at[c],
            dst_ref=recv_a.at[c],
            send_sem=a_ssem.at[c],
            recv_sem=a_rsem.at[c],
            device_id=sibling,
            device_id_type=MESH,
        )

    def cp_x(c, dx):
        return pltpu.make_async_remote_copy(
            src_ref=send_x.at[c, dx],
            dst_ref=recv_x.at[c, dx],
            send_sem=x_ssem.at[c, dx],
            recv_sem=x_rsem.at[c, dx],
            device_id=x_peer(dx),
            device_id_type=MESH,
        )

    def cp_z(c, dz):
        return pltpu.make_async_remote_copy(
            src_ref=send_z.at[c, dz],
            dst_ref=recv_z.at[c, dz],
            send_sem=z_ssem.at[c, dz],
            recv_sem=z_rsem.at[c, dz],
            device_id=z_peer(dz),
            device_id_type=MESH,
        )

    def project(c):
        down_copy(c).wait()
        down = down_buf[c].reshape(local_count * ff, CHUNK)
        y = jnp.dot(hidden[...], down, preferred_element_type=f32)
        send_a[c] = y[half:].astype(bf16)
        own_a[c] = y[:half]
        cp_a(c).start()

    def add_core(c):
        cp_a(c).wait_recv()
        y = own_a[c] + recv_a[c].astype(f32)
        own_x[c] = y[:chip_rows]
        for dx in range(1, n_x):
            send_x[c, dx] = y[dx * chip_rows : (dx + 1) * chip_rows].astype(bf16)
            cp_x(c, dx).start()

    put = lax.broadcasted_iota(jnp.int32, (n_z * SLAB, chip_rows), 0)
    take = lax.broadcasted_iota(jnp.int32, (n_z * SLAB, chip_rows), 1)
    source = lax.div(put, SLAB) * tok + lax.rem(put, tok)
    block = lax.rem(lax.div(put, tok), quarters)

    def add_x(c):
        y = own_x[c]
        for dx in range(1, n_x):
            cp_x(c, dx).wait_recv()
            y += recv_x[c, dx].astype(f32)
        y = y.astype(bf16)
        slabs = jnp.zeros((n_z * SLAB, piece), f32)
        for q in range(quarters):
            pick = jnp.where((take == source) & (block == q), 1.0, 0.0).astype(bf16)
            slabs += jnp.dot(pick, y[:, q * piece : (q + 1) * piece], preferred_element_type=f32)
        send_z[c] = slabs.astype(bf16).reshape(n_z, SLAB, piece)
        for dz in range(1, n_z):
            cp_z(c, dz).start()

    def finish(c):
        y = send_z[c, 0].astype(f32)
        for dz in range(1, n_z):
            cp_z(c, dz).wait_recv()
            y += recv_z[c, dz].astype(f32)
        for q in range(quarters):
            at = pl.multiple_of(c * CHUNK + q * piece, LANES)
            out[:, pl.ds(at, piece)] = y[q * tok : (q + 1) * tok].astype(bf16)

    def step(i, _):
        for lag, stage in ((0, project), (LAG, add_core), (2 * LAG, add_x), (3 * LAG, finish)):

            @pl.when((i >= lag) & (i < count + lag))
            def _():
                stage(i - lag)

        return 0

    lax.fori_loop(0, count + 3 * LAG, step, 0)

    def drain(c, _):
        cp_a(c).wait_send()
        for dx in range(1, n_x):
            cp_x(c, dx).wait_send()
        for dz in range(1, n_z):
            cp_z(c, dz).wait_send()
        return 0

    lax.fori_loop(0, count, drain, 0)


def body(
    tokens,
    routes,
    combine_weight,
    live_rows,
    gate_projection_weight,
    up_projection_weight,
    down_projection_weight,
):
    f32, bf16 = jnp.float32, jnp.bfloat16
    tok, width = tokens.shape
    n_dp = lax.axis_size("dp")
    n_z = lax.axis_size("expert")
    n_x = n_dp // 2
    local_count, _, ff = gate_projection_weight.shape
    quarters = SLAB // tok
    part = width // quarters
    count = width // CHUNK
    piece = CHUNK // quarters
    chip_rows = n_z * tok
    half = n_x * chip_rows
    total = 2 * half
    depth = min(2, local_count)
    vmem = pl.BlockSpec(memory_space=pltpu.VMEM)
    smem = pl.BlockSpec(memory_space=pltpu.SMEM)
    hbm = pl.BlockSpec(memory_space=pl.ANY)
    sem = pltpu.SemaphoreType.DMA
    weights = 3 * local_count * width * ff
    return pl.pallas_call(
        functools.partial(kernel, n_x, n_z, depth),
        out_shape=jax.ShapeDtypeStruct((tok, width), bf16),
        in_specs=[vmem, vmem, vmem, smem, hbm, hbm, hbm],
        out_specs=vmem,
        scratch_shapes=[
            pltpu.VMEM((total * quarters, part + LANES), bf16),
            pltpu.VMEM((quarters, total, part), bf16),
            pltpu.VMEM((total, LANES), f32),
            pltpu.VMEM((total, local_count * ff), bf16),
            pltpu.VMEM((total, ff), f32),
            pltpu.VMEM((total, ff), f32),
            pltpu.VMEM((depth, quarters, 2, part, ff), bf16),
            pltpu.VMEM((count, local_count, ff, CHUNK), bf16),
            pltpu.VMEM((count, half, CHUNK), f32),
            pltpu.VMEM((count, half, CHUNK), bf16),
            pltpu.VMEM((count, half, CHUNK), bf16),
            pltpu.VMEM((count, chip_rows, CHUNK), f32),
            pltpu.VMEM((count, n_x, chip_rows, CHUNK), bf16),
            pltpu.VMEM((count, n_x, chip_rows, CHUNK), bf16),
            pltpu.VMEM((count, n_z, SLAB, piece), bf16),
            pltpu.VMEM((count, n_z, SLAB, piece), bf16),
            sem((depth, quarters, 2)),
            sem((count,)),
            sem((n_z,)),
            sem((n_z,)),
            sem((n_x, n_z)),
            sem((n_x, n_z)),
            sem((n_x, n_z)),
            sem((n_x, n_z)),
            sem((count,)),
            sem((count,)),
            sem((count, n_x)),
            sem((count, n_x)),
            sem((count, n_z)),
            sem((count, n_z)),
        ],
        compiler_params=pltpu.CompilerParams(
            collective_id=0, has_side_effects=True, vmem_limit_bytes=64 * 1024 * 1024 - 65536
        ),
        cost_estimate=pl.CostEstimate(
            flops=2 * total * weights, bytes_accessed=2 * weights, transcendentals=total * ff * local_count
        ),
    )(
        tokens,
        routes,
        combine_weight,
        live_rows,
        gate_projection_weight,
        up_projection_weight,
        down_projection_weight,
    )


def solution(mesh):
    placed = (
        P(("groups", "expert", "dp"), None),
        P(("groups", "expert", "dp"), None),
        P(("groups", "expert", "dp"), None),
        P(("groups", "expert", "dp")),
        P("expert", None, "dp"),
        P("expert", None, "dp"),
        P("expert", "dp", None),
    )
    return jax.shard_map(
        body,
        mesh=mesh,
        in_specs=placed,
        out_specs=P(("groups", "expert", "dp"), None),
        check_vma=False,
    )
```

profile of v0, /device:TPU:0, one launch (start us, length us, event | category | flops | bytes accessed | tf_op | source)
XLA Modules:
  0.0 59.8 jit_solution(2412796606993241801)
XLA Ops:
  0.7 57.7 %shard_map.73 = bf16[4,7168]{1,0:T(4,128)(2,1)} custom-call(bf16[4,7168]{1,0:T(4,128)(2,1)} %tokens.1, s32[4,8]{1,0:T(4,128)} %routes.1, bf16[4,8]{1,0:T(4,128)(2,1)} %combine.1, s32[1]{0:T(128)S(6)} %copy.9.live, bf16[4,7168,512]{2,1,0:T(8,128)(2,1)} %gate_w.1, bf16[4,7168,512]{2,1,0:T(8,128)(2,1)} %up_w.1, bf16[4,512,7168]{2,1,0:T(8,128)(2,1)} %down_w.1), custom_call_target="tpu_custom_call" | custom-call | flops 5637144576 | bytes 88080384 | tf_op jit(solution)/shard_map/pallas_call | solution.py:353
  58.3 1.5 %copy.10 = bf16[4,7168]{1,0:T(4,128)(2,1)} copy(bf16[4,7168]{1,0:T(4,128)(2,1)} %shard_map.73) | data formatting | bytes 114688
where the time goes:
time: 60 us; the launch traced here: 59.8 us
  Pallas kernels  57.7 us (96%)
  local copies, waits for them, and re-layouts  1.46 us (2%)
  between operations  0.66 us (1%)
    pallas_call x1, Pallas kernels, body(): pl.pallas_call(functools.partial(kernel, n_x, n_z, depth), out_shape=jax....  57.7 us
    unnamed x1, local copies, waits for them, and re-layouts  1.46 us

commit v1 on v0

v1 whole, which is shorter than its diff:
```python
import functools

import jax
import jax.numpy as jnp
from jax import lax
from jax.experimental import pallas as pl
from jax.experimental.pallas import tpu as pltpu
from jax.sharding import PartitionSpec as P

SLAB = 16
CHUNK = 1024
HALVES = 2
BITES = 2
LANES = 128
LAG = 2
MESH = pl.DeviceIdType.MESH


def kernel(
    n_x,
    n_z,
    depth,
    tokens_hbm,
    routes_hbm,
    combine_hbm,
    live_hbm,
    gate_w,
    up_w,
    down_w,
    out,
    tokens,
    routes,
    combine,
    live,
    gathered_0,
    gathered_1,
    rows,
    table,
    hidden,
    acc,
    gu_ring,
    down_buf,
    own_a,
    send_a,
    recv_a,
    send_z,
    recv_z,
    in_sem,
    gu_sem,
    down_sem,
    gz_send,
    gz_recv,
    gx_send,
    gx_recv,
    gc_send,
    gc_recv,
    a_ssem,
    a_rsem,
    z_ssem,
    z_rsem,
):
    f32, bf16 = jnp.float32, jnp.bfloat16
    tok, width = tokens.shape
    top = routes.shape[1]
    local_count, ff = gate_w.shape[0], gate_w.shape[2]
    groups = SLAB // tok
    deep = width // HALVES
    part = deep // groups
    bite = deep // BITES
    count = width // CHUNK
    piece = CHUNK // groups
    chip_rows = n_z * tok
    total = 2 * n_x * chip_rows
    units = HALVES * local_count

    z = lax.axis_index("expert")
    dp = lax.axis_index("dp")
    core = lax.rem(dp, 2)
    x = lax.div(dp, 2)

    def dp_peer(c, dx):
        place = lax.rem(x + dx, n_x) * 2
        return {"dp": place + (1 - core if c else core)}

    def z_peer(dz):
        return {"expert": lax.rem(z + dz, n_z)}

    def slab(h, c, dx, dz):
        at = pl.ds(((c * n_x + dx) * n_z + dz) * SLAB, SLAB)
        return (gathered_0, gathered_1)[h].at[at, :]

    barrier = pltpu.get_barrier_semaphore()
    others = [(c, dx) for dx in range(n_x) for c in range(2) if c or dx]
    peers = [dp_peer(c, dx) for c, dx in others]
    peers += [z_peer(dz) for dz in range(1, n_z)]
    for peer in peers:
        pl.semaphore_signal(barrier, inc=1, device_id=peer, device_id_type=MESH)

    inputs = [
        pltpu.make_async_copy(source, target, in_sem.at[i])
        for i, (source, target) in enumerate(
            (
                (tokens_hbm, tokens),
                (routes_hbm, routes),
                (combine_hbm, combine),
                (live_hbm, live),
            )
        )
    ]
    for copy in inputs:
        copy.start()

    def gu_copy(t, b, which):
        place = lax.rem(t, depth)
        h = lax.div(t, local_count)
        e = lax.rem(t, local_count)
        begin = pl.multiple_of(h * deep + b * bite, SLAB)
        return pltpu.make_async_copy(
            (gate_w, up_w)[which].at[e, pl.ds(begin, bite), :],
            gu_ring.at[place, which, b],
            gu_sem.at[place, which, b],
        )

    def down_copy(c):
        return pltpu.make_async_copy(
            down_w.at[:, :, pl.ds(pl.multiple_of(c * CHUNK, CHUNK), CHUNK)],
            down_buf.at[c],
            down_sem.at[c],
        )

    for t in range(depth):
        for b in range(BITES):
            for which in range(2):
                gu_copy(t, b, which).start()

    for copy in inputs:
        copy.wait()

    wide = tokens[...].astype(f32)
    for h, target in enumerate((gathered_0, gathered_1)):
        cut = [wide[:, h * deep + g * part : h * deep + (g + 1) * part] for g in range(groups)]
        target[0:SLAB, 0:part] = jnp.concatenate(cut, axis=0).astype(bf16)
    lane = lax.broadcasted_iota(jnp.int32, (tok, LANES), 1)
    row = lax.broadcasted_iota(jnp.int32, (tok, LANES), 0)
    chosen = routes[...]
    share = combine[...].astype(f32)
    weights = jnp.zeros((tok, LANES), f32)
    for k in range(top):
        weights += jnp.where(chosen[:, k : k + 1] == lane, share[:, k : k + 1], 0.0)
    weights = jnp.where(row < live[...], weights, 0.0)
    gathered_0[0:SLAB, part : part + LANES] = jnp.concatenate([weights] * groups, axis=0).astype(bf16)

    pl.semaphore_wait(barrier, len(peers))

    def gz(h, dz):
        return pltpu.make_async_remote_copy(
            src_ref=slab(h, 0, 0, 0),
            dst_ref=slab(h, 0, 0, n_z - dz),
            send_sem=gz_send.at[h, dz],
            recv_sem=gz_recv.at[h, n_z - dz],
            device_id=z_peer(dz),
            device_id_type=MESH,
        )

    def gx(h, dx, dz):
        return pltpu.make_async_remote_copy(
            src_ref=slab(h, 0, 0, dz),
            dst_ref=slab(h, 0, n_x - dx, dz),
            send_sem=gx_send.at[h, dx, dz],
            recv_sem=gx_recv.at[h, n_x - dx, dz],
            device_id=dp_peer(0, dx),
            device_id_type=MESH,
        )

    def gc(h, dx, dz):
        return pltpu.make_async_remote_copy(
            src_ref=slab(h, 0, dx, dz),
            dst_ref=slab(h, 1, dx, dz),
            send_sem=gc_send.at[h, dx, dz],
            recv_sem=gc_recv.at[h, dx, dz],
            device_id=dp_peer(1, 0),
            device_id_type=MESH,
        )

    order = sorted(range(1, n_z), key=lambda dz: (min(dz, n_z - dz), dz))

    def spread_z(h):
        for dz in order:
            gz(h, dz).start()
        for dx in range(1, n_x):
            gx(h, dx, 0).start()
        gc(h, 0, 0).start()

    def spread_x(h):
        for dz in order:
            gz(h, n_z - dz).wait_recv()
            for dx in range(1, n_x):
                gx(h, dx, dz).start()
            gc(h, 0, dz).start()

    def spread_core(h):
        for dz in [0] + order:
            for dx in range(1, n_x):
                gx(h, n_x - dx, dz).wait_recv()
                gc(h, dx, dz).start()

    def whole_rows(h):
        for dz in [0] + order:
            for dx in range(n_x):
                gc(h, dx, dz).wait_recv()
        to = lax.broadcasted_iota(jnp.int32, (total, total * groups), 0)
        came = lax.broadcasted_iota(jnp.int32, (total, total * groups), 1)
        first = lax.div(to, tok) * SLAB + lax.rem(to, tok)
        source = (gathered_0, gathered_1)[h]
        for g in range(groups):
            pick = jnp.where(came == first + g * tok, 1.0, 0.0).astype(bf16)
            if g == 0 and h == 0:
                both = jnp.dot(pick, source[...], preferred_element_type=f32)
                table[...] = both[:, part:]
                both = both[:, :part]
            else:
                both = jnp.dot(pick, source[:, :part], preferred_element_type=f32)
            rows[h, :, g * part : (g + 1) * part] = both.astype(bf16)

    steps = min(depth, units) * BITES
    spread = -(-count // steps)

    def multiply(h, e):
        t = h * local_count + e
        place = lax.rem(t, depth)
        for b in range(BITES):
            for which in range(2):
                gu_copy(t, b, which).wait()
                term = jnp.dot(
                    rows[h, :, b * bite : (b + 1) * bite],
                    gu_ring[place, which, b],
                    preferred_element_type=f32,
                )
                if b == 0 and h == 0:
                    acc[e, which] = term
                else:
                    acc[e, which] += term

            @pl.when(t + depth < units)
            def _():
                for which in range(2):
                    gu_copy(t + depth, b, which).start()

            @pl.when(t + depth >= units)
            def _():
                begin = ((t + depth - units) * BITES + b) * spread
                for k in range(spread):

                    @pl.when(begin + k < count)
                    def _():
                        down_copy(begin + k).start()

    def activate(e):
        lanes = lax.broadcasted_iota(jnp.int32, (total, LANES), 1)
        mine = jnp.where(lanes == z * local_count + e, table[...], 0.0)
        weight = jnp.sum(mine, axis=1, keepdims=True)
        g = acc[e, 0]
        value = g / (1.0 + jnp.exp(-g)) * acc[e, 1] * weight
        hidden[:, pl.ds(pl.multiple_of(e * ff, LANES), ff)] = value.astype(bf16)

    spread_z(0)
    spread_x(0)
    spread_z(1)
    spread_core(0)
    whole_rows(0)

    def first_half(e, _):
        multiply(0, e)

        @pl.when(e == 0)
        def _():
            spread_x(1)

        @pl.when(e == min(1, local_count - 1))
        def _():
            spread_core(1)

        return 0

    lax.fori_loop(0, local_count, first_half, 0)
    whole_rows(1)

    def second_half(e, _):
        multiply(1, e)
        activate(e)
        return 0

    lax.fori_loop(0, local_count, second_half, 0)

    def cp_a(c, i):
        return pltpu.make_async_remote_copy(
            src_ref=send_a.at[c, i],
            dst_ref=recv_a.at[c, i],
            send_sem=a_ssem.at[c, i],
            recv_sem=a_rsem.at[c, i],
            device_id=dp_peer(*others[i]),
            device_id_type=MESH,
        )

    def cp_z(c, dz):
        return pltpu.make_async_remote_copy(
            src_ref=send_z.at[c, dz],
            dst_ref=recv_z.at[c, dz],
            send_sem=z_ssem.at[c, dz],
            recv_sem=z_rsem.at[c, dz],
            device_id=z_peer(dz),
            device_id_type=MESH,
        )

    def project(c):
        down_copy(c).wait()
        down = down_buf[c].reshape(local_count * ff, CHUNK)
        y = jnp.dot(hidden[...], down, preferred_element_type=f32)
        own_a[c] = y[:chip_rows]
        for i, (k, dx) in enumerate(others):
            at = (k * n_x + dx) * chip_rows
            send_a[c, i] = y[at : at + chip_rows].astype(bf16)
        for i in reversed(range(len(others))):
            cp_a(c, i).start()

    def add_dp(c):
        y = own_a[c]
        for i in range(len(others)):
            cp_a(c, i).wait_recv()
            y += recv_a[c, i].astype(f32)
        for dz in range(n_z):
            cut = y[dz * tok : (dz + 1) * tok]
            cut = [cut[:, g * piece : (g + 1) * piece] for g in range(groups)]
            send_z[c, dz] = jnp.concatenate(cut, axis=0).astype(bf16)
        for dz in order:
            cp_z(c, dz).start()

    def finish(c):
        y = send_z[c, 0].astype(f32)
        for dz in range(1, n_z):
            cp_z(c, dz).wait_recv()
            y += recv_z[c, dz].astype(f32)
        for g in range(groups):
            at = pl.multiple_of(c * CHUNK + g * piece, LANES)
            out[:, pl.ds(at, piece)] = y[g * tok : (g + 1) * tok].astype(bf16)

    def step(i, _):
        for lag, stage in ((0, project), (LAG, add_dp), (2 * LAG, finish)):

            @pl.when((i >= lag) & (i < count + lag))
            def _():
                stage(i - lag)

        return 0

    lax.fori_loop(0, count + 2 * LAG, step, 0)

    for h in range(HALVES):
        for dz in range(n_z):
            if dz:
                gz(h, dz).wait_send()
            for dx in range(n_x):
                if dx:
                    gx(h, dx, dz).wait_send()
                gc(h, dx, dz).wait_send()

    def drain(c, _):
        for i in range(len(others)):
            cp_a(c, i).wait_send()
        for dz in range(1, n_z):
            cp_z(c, dz).wait_send()
        return 0

    lax.fori_loop(0, count, drain, 0)


def body(
    tokens,
    routes,
    combine_weight,
    live_rows,
    gate_projection_weight,
    up_projection_weight,
    down_projection_weight,
):
    f32, bf16 = jnp.float32, jnp.bfloat16
    tok, width = tokens.shape
    top = routes.shape[1]
    n_dp = lax.axis_size("dp")
    n_z = lax.axis_size("expert")
    n_x = n_dp // 2
    local_count, _, ff = gate_projection_weight.shape
    groups = SLAB // tok
    deep = width // HALVES
    part = deep // groups
    count = width // CHUNK
    piece = CHUNK // groups
    chip_rows = n_z * tok
    total = n_dp * chip_rows
    depth = min(4, HALVES * local_count)
    vmem = pl.BlockSpec(memory_space=pltpu.VMEM)
    hbm = pl.BlockSpec(memory_space=pl.ANY)
    sem = pltpu.SemaphoreType.DMA
    weights = 3 * local_count * width * ff
    return pl.pallas_call(
        functools.partial(kernel, n_x, n_z, depth),
        out_shape=jax.ShapeDtypeStruct((tok, width), bf16),
        in_specs=[hbm] * 7,
        out_specs=vmem,
        scratch_shapes=[
            pltpu.VMEM((tok, width), bf16),
            pltpu.VMEM((tok, top), jnp.int32),
            pltpu.VMEM((tok, top), bf16),
            pltpu.VMEM((1, 1), jnp.int32),
            pltpu.VMEM((total * groups, part + LANES), bf16),
            pltpu.VMEM((total * groups, part), bf16),
            pltpu.VMEM((HALVES, total, deep), bf16),
            pltpu.VMEM((total, LANES), f32),
            pltpu.VMEM((total, local_count * ff), bf16),
            pltpu.VMEM((local_count, 2, total, ff), f32),
            pltpu.VMEM((depth, 2, BITES, deep // BITES, ff), bf16),
            pltpu.VMEM((count, local_count, ff, CHUNK), bf16),
            pltpu.VMEM((count, chip_rows, CHUNK), f32),
            pltpu.VMEM((count, n_dp - 1, chip_rows, CHUNK), bf16),
            pltpu.VMEM((count, n_dp - 1, chip_rows, CHUNK), bf16),
            pltpu.VMEM((count, n_z, SLAB, piece), bf16),
            pltpu.VMEM((count, n_z, SLAB, piece), bf16),
            sem((4,)),
            sem((depth, 2, BITES)),
            sem((count,)),
            sem((HALVES, n_z)),
            sem((HALVES, n_z)),
            sem((HALVES, n_x, n_z)),
            sem((HALVES, n_x, n_z)),
            sem((HALVES, n_x, n_z)),
            sem((HALVES, n_x, n_z)),
            sem((count, n_dp - 1)),
            sem((count, n_dp - 1)),
            sem((count, n_z)),
            sem((count, n_z)),
        ],
        compiler_params=pltpu.CompilerParams(
            collective_id=0, has_side_effects=True, vmem_limit_bytes=64 * 1024 * 1024 - 65536
        ),
        cost_estimate=pl.CostEstimate(
            flops=2 * total * weights, bytes_accessed=2 * weights, transcendentals=total * ff * local_count
        ),
    )(
        tokens,
        routes,
        combine_weight,
        live_rows.reshape(1, 1),
        gate_projection_weight,
        up_projection_weight,
        down_projection_weight,
    )


def solution(mesh):
    placed = (
        P(("groups", "expert", "dp"), None),
        P(("groups", "expert", "dp"), None),
        P(("groups", "expert", "dp"), None),
        P(("groups", "expert", "dp")),
        P("expert", None, "dp"),
        P("expert", None, "dp"),
        P("expert", "dp", None),
    )
    return jax.shard_map(
        body,
        mesh=mesh,
        in_specs=placed,
        out_specs=P(("groups", "expert", "dp"), None),
        check_vma=False,
    )
```

time: 60 us -> 51.2 us (0.85)
  Pallas kernels: 57.7 us -> 49 us
    pallas_call x1, Pallas kernels: 57.7 us -> 49 us  [body(): pl.pallas_call(functools.partial(kernel, n_x, n_z, depth), out_shape=jax....]
where the time goes in v1:
time: 51.2 us; the launch traced here: 51.1 us
  Pallas kernels  49 us (96%)
  local copies, waits for them, and re-layouts  1.46 us (3%)
  between operations  0.66 us (1%)
    pallas_call x1, Pallas kernels, body(): pl.pallas_call(functools.partial(kernel, n_x, n_z, depth), out_shape=jax....  49 us
    unnamed x1, local copies, waits for them, and re-layouts  1.46 us

profile of v1, /device:TPU:0, one launch (start us, length us, event | category | flops | bytes accessed | tf_op | source)
XLA Modules:
  0.0 51.1 jit_solution(12363775142666713395)
XLA Ops:
  0.7 49.0 %shard_map.73 = bf16[4,7168]{1,0:T(4,128)(2,1)} custom-call(bf16[4,7168]{1,0:T(4,128)(2,1)} %tokens_hbm.1, s32[4,8]{1,0:T(4,128)} %routes_hbm.1, bf16[4,8]{1,0:T(4,128)(2,1)} %combine_hbm.1, s32[1,1]{1,0:T(1,128)} %bitcast.1.live_hbm, bf16[4,7168,512]{2,1,0:T(8,128)(2,1)} %gate_w.1, bf16[4,7168,512]{2,1,0:T(8,128)(2,1)} %up_w.1, bf16[4,512,7168]{2,1,0:T(8,128)(2,1)} %down_w.1), custom_call_target="tpu_custom_call" | custom-call | flops 5637144576 | bytes 88080384 | tf_op jit(solution)/shard_map/pallas_call | solution.py:405
  49.6 1.5 %copy.10 = bf16[4,7168]{1,0:T(4,128)(2,1)} copy(bf16[4,7168]{1,0:T(4,128)(2,1)} %shard_map.73) | data formatting | bytes 114688

commit v2 on v1

--- a/solution.py
+++ b/solution.py
@@ -12,7 +12,7 @@
 HALVES = 2
 BITES = 2
 LANES = 128
-LAG = 2
+LAGS = (0, 2, 5, 8)
 MESH = pl.DeviceIdType.MESH
 
 
@@ -43,6 +43,8 @@
     own_a,
     send_a,
     recv_a,
+    send_x,
+    recv_x,
     send_z,
     recv_z,
     in_sem,
@@ -56,6 +58,8 @@
     gc_recv,
     a_ssem,
     a_rsem,
+    x_ssem,
+    x_rsem,
     z_ssem,
     z_rsem,
 ):
@@ -70,7 +74,8 @@
     count = width // CHUNK
     piece = CHUNK // groups
     chip_rows = n_z * tok
-    total = 2 * n_x * chip_rows
+    half = n_x * chip_rows
+    total = 2 * half
     units = HALVES * local_count
 
     z = lax.axis_index("expert")
@@ -90,8 +95,8 @@
         return (gathered_0, gathered_1)[h].at[at, :]
 
     barrier = pltpu.get_barrier_semaphore()
-    others = [(c, dx) for dx in range(n_x) for c in range(2) if c or dx]
-    peers = [dp_peer(c, dx) for c, dx in others]
+    peers = [dp_peer(1, 0)]
+    peers += [dp_peer(0, dx) for dx in range(1, n_x)]
     peers += [z_peer(dz) for dz in range(1, n_z)]
     for peer in peers:
         pl.semaphore_signal(barrier, inc=1, device_id=peer, device_id_type=MESH)
@@ -210,7 +215,8 @@
                 gc(h, dx, dz).wait_recv()
         to = lax.broadcasted_iota(jnp.int32, (total, total * groups), 0)
         came = lax.broadcasted_iota(jnp.int32, (total, total * groups), 1)
-        first = lax.div(to, tok) * SLAB + lax.rem(to, tok)
+        within = to & (tok - 1)
+        first = (to - within) * groups + within
         source = (gathered_0, gathered_1)[h]
         for g in range(groups):
             pick = jnp.where(came == first + g * tok, 1.0, 0.0).astype(bf16)
@@ -292,13 +298,23 @@
 
     lax.fori_loop(0, local_count, second_half, 0)
 
-    def cp_a(c, i):
+    def cp_a(c):
         return pltpu.make_async_remote_copy(
-            src_ref=send_a.at[c, i],
-            dst_ref=recv_a.at[c, i],
-            send_sem=a_ssem.at[c, i],
-            recv_sem=a_rsem.at[c, i],
-            device_id=dp_peer(*others[i]),
+            src_ref=send_a.at[c],
+            dst_ref=recv_a.at[c],
+            send_sem=a_ssem.at[c],
+            recv_sem=a_rsem.at[c],
+            device_id=dp_peer(1, 0),
+            device_id_type=MESH,
+        )
+
+    def cp_x(c, dx):
+        return pltpu.make_async_remote_copy(
+            src_ref=send_x.at[c, dx - 1],
+            dst_ref=recv_x.at[c, dx - 1],
+            send_sem=x_ssem.at[c, dx - 1],
+            recv_sem=x_rsem.at[c, dx - 1],
+            device_id=dp_peer(0, dx),
             device_id_type=MESH,
         )
 
@@ -316,18 +332,23 @@
         down_copy(c).wait()
         down = down_buf[c].reshape(local_count * ff, CHUNK)
         y = jnp.dot(hidden[...], down, preferred_element_type=f32)
-        own_a[c] = y[:chip_rows]
-        for i, (k, dx) in enumerate(others):
-            at = (k * n_x + dx) * chip_rows
-            send_a[c, i] = y[at : at + chip_rows].astype(bf16)
-        for i in reversed(range(len(others))):
-            cp_a(c, i).start()
-
-    def add_dp(c):
-        y = own_a[c]
-        for i in range(len(others)):
-            cp_a(c, i).wait_recv()
-            y += recv_a[c, i].astype(f32)
+        send_a[c] = y[half:].astype(bf16)
+        cp_a(c).start()
+        own_a[c] = y[:half]
+
+    def add_core(c):
+        cp_a(c).wait_recv()
+        for dx in range(1, n_x):
+            at = slice(dx * chip_rows, (dx + 1) * chip_rows)
+            send_x[c, dx - 1] = (own_a[c, at] + recv_a[c, at].astype(f32)).astype(bf16)
+            cp_x(c, dx).start()
+        own_a[c, :chip_rows] += recv_a[c, :chip_rows].astype(f32)
+
+    def add_x(c):
+        y = own_a[c, :chip_rows]
+        for dx in range(1, n_x):
+            cp_x(c, dx).wait_recv()
+            y += recv_x[c, dx - 1].astype(f32)
         for dz in range(n_z):
             cut = y[dz * tok : (dz + 1) * tok]
             cut = [cut[:, g * piece : (g + 1) * piece] for g in range(groups)]
@@ -345,7 +366,7 @@
             out[:, pl.ds(at, piece)] = y[g * tok : (g + 1) * tok].astype(bf16)
 
     def step(i, _):
-        for lag, stage in ((0, project), (LAG, add_dp), (2 * LAG, finish)):
+        for lag, stage in zip(LAGS, (project, add_core, add_x, finish)):
 
             @pl.when((i >= lag) & (i < count + lag))
             def _():
@@ -353,7 +374,7 @@
 
         return 0
 
-    lax.fori_loop(0, count + 2 * LAG, step, 0)
+    lax.fori_loop(0, count + LAGS[-1], step, 0)
 
     for h in range(HALVES):
         for dz in range(n_z):
@@ -365,8 +386,9 @@
                 gc(h, dx, dz).wait_send()
 
     def drain(c, _):
-        for i in range(len(others)):
-            cp_a(c, i).wait_send()
+        cp_a(c).wait_send()
+        for dx in range(1, n_x):
+            cp_x(c, dx).wait_send()
         for dz in range(1, n_z):
             cp_z(c, dz).wait_send()
         return 0
@@ -396,7 +418,8 @@
     count = width // CHUNK
     piece = CHUNK // groups
     chip_rows = n_z * tok
-    total = n_dp * chip_rows
+    half = n_x * chip_rows
+    total = 2 * half
     depth = min(4, HALVES * local_count)
     vmem = pl.BlockSpec(memory_space=pltpu.VMEM)
     hbm = pl.BlockSpec(memory_space=pl.ANY)
@@ -420,9 +443,11 @@
             pltpu.VMEM((local_count, 2, total, ff), f32),
             pltpu.VMEM((depth, 2, BITES, deep // BITES, ff), bf16),
             pltpu.VMEM((count, local_count, ff, CHUNK), bf16),
-            pltpu.VMEM((count, chip_rows, CHUNK), f32),
-            pltpu.VMEM((count, n_dp - 1, chip_rows, CHUNK), bf16),
-            pltpu.VMEM((count, n_dp - 1, chip_rows, CHUNK), bf16),
+            pltpu.VMEM((count, half, CHUNK), f32),
+            pltpu.VMEM((count, half, CHUNK), bf16),
+            pltpu.VMEM((count, half, CHUNK), bf16),
+            pltpu.VMEM((count, n_x - 1, chip_rows, CHUNK), bf16),
+            pltpu.VMEM((count, n_x - 1, chip_rows, CHUNK), bf16),
             pltpu.VMEM((count, n_z, SLAB, piece), bf16),
             pltpu.VMEM((count, n_z, SLAB, piece), bf16),
             sem((4,)),
@@ -434,8 +459,10 @@
             sem((HALVES, n_x, n_z)),
             sem((HALVES, n_x, n_z)),
             sem((HALVES, n_x, n_z)),
-            sem((count, n_dp - 1)),
-            sem((count, n_dp - 1)),
+            sem((count,)),
+            sem((count,)),
+            sem((count, n_x - 1)),
+            sem((count, n_x - 1)),
             sem((count, n_z)),
             sem((count, n_z)),
         ],

time: 51.2 us -> 48 us (0.938)
  Pallas kernels: 49 us -> 45.7 us
    pallas_call x1, Pallas kernels: 49 us -> 45.7 us  [body(): pl.pallas_call(functools.partial(kernel, n_x, n_z, depth), out_shape=jax....]
where the time goes in v2:
time: 48 us; the launch traced here: 47.9 us
  Pallas kernels  45.7 us (95%)
  local copies, waits for them, and re-layouts  1.46 us (3%)
  between operations  0.66 us (1%)
    pallas_call x1, Pallas kernels, body(): pl.pallas_call(functools.partial(kernel, n_x, n_z, depth), out_shape=jax....  45.7 us
    unnamed x1, local copies, waits for them, and re-layouts  1.46 us

profile of v2, /device:TPU:0, one launch (start us, length us, event | category | flops | bytes accessed | tf_op | source)
XLA Modules:
  0.0 47.9 jit_solution(7611812529887482322)
XLA Ops:
  0.7 45.7 %shard_map.73 = bf16[4,7168]{1,0:T(4,128)(2,1)} custom-call(bf16[4,7168]{1,0:T(4,128)(2,1)} %tokens_hbm.1, s32[4,8]{1,0:T(4,128)} %routes_hbm.1, bf16[4,8]{1,0:T(4,128)(2,1)} %combine_hbm.1, s32[1,1]{1,0:T(1,128)} %bitcast.1.live_hbm, bf16[4,7168,512]{2,1,0:T(8,128)(2,1)} %gate_w.1, bf16[4,7168,512]{2,1,0:T(8,128)(2,1)} %up_w.1, bf16[4,512,7168]{2,1,0:T(8,128)(2,1)} %down_w.1), custom_call_target="tpu_custom_call" | custom-call | flops 5637144576 | bytes 88080384 | tf_op jit(solution)/shard_map/pallas_call | solution.py:428
  46.4 1.5 %copy.10 = bf16[4,7168]{1,0:T(4,128)(2,1)} copy(bf16[4,7168]{1,0:T(4,128)(2,1)} %shard_map.73) | data formatting | bytes 114688
